TPU v7x, 32 devices: a whole 2x2x4 slice. The times are simulated.
32 devices in a mesh: slot: 2 (over y), seq: 16 (over z, x, core).
Axes of the slice: x: 2, y: 2, z: 4, core: 2. Of those that a mesh axis runs over, the one named last changes fastest.
Arguments:
- hidden: bfloat16 [2, 2, 2048, 768], P('slot', None, 'seq'), may hold values from -6 to 6
- out_grad: bfloat16 [2, 2, 2048, 768], P('slot', None, 'seq'), may hold values from -6 to 6
- lengths: int32 [2, 2], P('slot'), may hold values from 512 to 2048, as said below
- w_in: bfloat16 [768, 1536], P(('slot', 'seq')), may hold values from -0.21875 to 0.21875
- w_depth: bfloat16 [9, 768], P(None, ('slot', 'seq')), may hold values from -2 to 2
- w_point: bfloat16 [768, 384], P(('slot', 'seq')), may hold values from -0.21875 to 0.21875
- w_kern: bfloat16 [20736], P(('slot', 'seq')), may hold values from -0.3125 to 0.3125
- w_out: bfloat16 [768, 768], P(('slot', 'seq')), may hold values from -0.625 to 0.625
- ln_gain: bfloat16 [2, 768], P(None, ('slot', 'seq')), may hold values from 0.099609375 to 1.8984375
- ln_bias: bfloat16 [2, 768], P(None, ('slot', 'seq')), may hold values from -3 to 3
- w_up: bfloat16 [2, 384, 1536], P(None, None, ('slot', 'seq')), may hold values from -0.3125 to 0.3125
- w_down: bfloat16 [2, 1536, 384], P(None, ('slot', 'seq')), may hold values from -0.15625 to 0.15625
Outputs:
- output: bfloat16 [2, 2, 2048, 768], P('slot', None, 'seq')
- hidden_grad: bfloat16 [2, 2, 2048, 768], P('slot', None, 'seq')
- w_in_grad: float32 [768, 1536], P(('slot', 'seq'))
- w_depth_grad: float32 [9, 768], P(None, ('slot', 'seq'))
- w_point_grad: float32 [768, 384], P(('slot', 'seq'))
- w_kern_grad: float32 [20736], P(('slot', 'seq'))
- w_out_grad: float32 [768, 768], P(('slot', 'seq'))
- ln_gain_grad: float32 [2, 768], P(None, ('slot', 'seq'))
- ln_bias_grad: float32 [2, 768], P(None, ('slot', 'seq'))
- w_up_grad: float32 [2, 384, 1536], P(None, None, ('slot', 'seq'))
- w_down_grad: float32 [2, 1536, 384], P(None, ('slot', 'seq'))
Inputs may be any that keep to these rules, and one draw needn't show every extreme that they name: lengths[s, b] valid positions open sequence b of slot s; in every draw one sequence has all 2048.
All inputs are finite; a program needn't handle non-finite values.
Results may differ from a plain program's by a relative error of at most 0.017.
Values may be sent and summed in bfloat16 or wider, within the bound.
No kernel may reach another device: no remote copies, remote signals or barrier semaphores. Data moves between devices by JAX's collectives and lax.ppermute only.
A program may use at most 192 MiB of HBM per device.

v0:
```python
import math

import jax
import jax.numpy as jnp
from jax import lax
from jax.sharding import PartitionSpec as P

D = 768
HEADS = 6
HEAD_DIM = 64
KSIZE = 9
GROUPS = 2
DA = 384


norm_eps = 1e-12
neg_fill = -1e30


def extended_2(block, sides, width):
    for axis, dim in sides:
        count = lax.axis_size(axis)
        forward = [(i, i + 1) for i in range(count - 1)]
        backward = [(target, source) for source, target in forward]
        low = lax.ppermute(
            lax.slice_in_dim(block, block.shape[dim] - width, None, axis=dim), axis, forward
        )
        high = lax.ppermute(lax.slice_in_dim(block, 0, width, axis=dim), axis, backward)
        block = jnp.concatenate([low, block, high], axis=dim)
    return block


def rounded(value):
    return lax.optimization_barrier(value.astype(jnp.bfloat16)).astype(jnp.float32)


def low(value):
    return value - lax.stop_gradient(value) + lax.stop_gradient(rounded(value))


def normalize_rows(scores):
    top = jnp.max(scores, axis=-1, keepdims=True)
    expo = jnp.exp(scores - top)
    return expo / jnp.sum(expo, axis=-1, keepdims=True)


def layer_norm(value, gain, shift):
    centre = value - jnp.mean(value, axis=-1, keepdims=True)
    spread = jnp.mean(centre * centre, axis=-1, keepdims=True)
    return centre * lax.rsqrt(spread + norm_eps) * gain + shift


def widen(pieces):
    return tuple((piece.astype(jnp.float32) for piece in pieces))


def front(masked, w_in):
    return low(jnp.dot(masked, w_in, preferred_element_type=jnp.float32))


def conv_key(masked_ext, w_depth, w_point):
    width = w_depth.shape[0]
    length = masked_ext.shape[0] - width + 1
    depth_out = low(sum((w_depth[j] * masked_ext[j : j + length] for j in range(width))))
    return jnp.dot(depth_out, w_point, preferred_element_type=jnp.float32)


def conv_logits(key_conv, query, w_kern):
    mixed = low(key_conv * query)
    return jnp.dot(
        mixed, w_kern.reshape(query.shape[1], HEADS * KSIZE), preferred_element_type=jnp.float32
    )


def conv_mix(logits, conv_ext):
    length = logits.shape[0]
    kernel = normalize_rows(logits.reshape(length, HEADS, KSIZE))
    conv_heads = conv_ext.reshape(conv_ext.shape[0], HEADS, HEAD_DIM)
    context_c = sum((kernel[:, :, j, None] * conv_heads[j : j + length] for j in range(KSIZE)))
    return context_c.reshape(length, DA)


def end_branch(context, w_out):
    return jnp.dot(context, w_out, preferred_element_type=jnp.float32)


def end_first(branch, tokens, gain, shift, w_up):
    length = tokens.shape[0]
    first = layer_norm(tokens + branch, gain[0], shift[0])
    grouped = low(first).reshape(length, GROUPS, D // GROUPS)
    inner = jnp.einsum("sgi,gio->sgo", grouped, w_up, preferred_element_type=jnp.float32)
    return (first, inner)


def end_down(inner, w_down):
    length = inner.shape[0]
    active = low(0.5 * inner * (1.0 + lax.erf(inner * 0.7071067811865476)))
    return jnp.einsum("sgo,goi->sgi", active, w_down, preferred_element_type=jnp.float32).reshape(
        length, D
    )


def end_out(first, down, gain, shift):
    return layer_norm(first + down, gain[1], shift[1])


def fold_rims(extended, received, half, length):
    core = extended[half : half + length]
    head_part = jnp.pad(received[:half], ((0, length - half), (0, 0)))
    tail_part = jnp.pad(received[-half:], ((length - half, 0), (0, 0)))
    return core + head_part + tail_part


def attend_back(query_heads, key_all, value_all, d_context, context, lse, seq_len, scale):
    total_rows = key_all.shape[0]
    length = query_heads.shape[0]
    block = math.gcd(total_rows, 1024)
    grad_heads = d_context.reshape(length, HEADS, HEAD_DIM).transpose(1, 0, 2).astype(jnp.bfloat16)
    delta = jnp.sum((d_context * context).reshape(length, HEADS, HEAD_DIM), axis=2).T

    def one_block(d_query, start):
        key_blk = lax.dynamic_slice_in_dim(key_all, start, block, 0).reshape(block, HEADS, HEAD_DIM)
        value_blk = lax.dynamic_slice_in_dim(value_all, start, block, 0).reshape(
            block, HEADS, HEAD_DIM
        )
        scores = (
            jnp.einsum("qhd,khd->hqk", query_heads, key_blk, preferred_element_type=jnp.float32)
            * scale
        )
        valid = start + jnp.arange(block, dtype=jnp.int32) < seq_len
        scores = jnp.where(valid[None, None, :], scores, neg_fill)
        probs = jnp.exp(scores - lse[:, :, None])
        d_values_blk = jnp.einsum(
            "hqk,hqd->khd",
            probs.astype(jnp.bfloat16),
            grad_heads,
            preferred_element_type=jnp.float32,
        )
        d_probs = jnp.einsum(
            "hqd,khd->hqk", grad_heads, value_blk, preferred_element_type=jnp.float32
        )
        d_scores = (probs * (d_probs - delta[:, :, None])).astype(jnp.bfloat16)
        d_query = (
            d_query
            + jnp.einsum("hqk,khd->qhd", d_scores, key_blk, preferred_element_type=jnp.float32)
            * scale
        )
        d_keys_blk = (
            jnp.einsum("hqk,qhd->khd", d_scores, query_heads, preferred_element_type=jnp.float32)
            * scale
        )
        return (d_query, (d_keys_blk.reshape(block, DA), d_values_blk.reshape(block, DA)))

    starts = jnp.arange(total_rows // block, dtype=jnp.int32) * block
    d_query, (d_keys, d_values) = lax.scan(
        one_block, jnp.zeros((length, HEADS, HEAD_DIM), jnp.float32), starts
    )
    return (
        d_query.reshape(length, DA),
        d_keys.reshape(total_rows, DA),
        d_values.reshape(total_rows, DA),
    )


def per_device(
    hidden, out_grad, lengths, w_in, w_depth, w_point, w_kern, w_out, ln_gain, ln_bias, w_up, w_down
):
    shards = (w_in, w_depth, w_point, w_kern, w_out, ln_gain, ln_bias, w_up, w_down)
    micro = hidden.shape[1]
    length = hidden.shape[2]
    half = w_depth.shape[0] // 2
    scale = HEAD_DIM ** (-0.5)
    key_start = lax.axis_index("seq") * length
    positions = key_start + jnp.arange(length, dtype=jnp.int32)
    totals = None
    results = []
    token_grads = []
    for index in range(micro):
        params = widen(
            (
                lax.all_gather(shards[0], ("slot", "seq"), axis=0, tiled=True),
                lax.all_gather(shards[1], ("slot", "seq"), axis=1, tiled=True),
                lax.all_gather(shards[2], ("slot", "seq"), axis=0, tiled=True),
                lax.all_gather(shards[3], ("slot", "seq"), axis=0, tiled=True),
                lax.all_gather(shards[4], ("slot", "seq"), axis=0, tiled=True),
                lax.all_gather(shards[5], ("slot", "seq"), axis=1, tiled=True),
                lax.all_gather(shards[6], ("slot", "seq"), axis=1, tiled=True),
                lax.all_gather(shards[7], ("slot", "seq"), axis=2, tiled=True),
                lax.all_gather(shards[8], ("slot", "seq"), axis=1, tiled=True),
            )
        )
        w_in_f, w_depth_f, w_point_f, w_kern_f, w_out_f, gain_f, bias_f, w_up_f, w_down_f = params
        seq_len = lengths[0, index]
        mask = (positions < seq_len).astype(jnp.float32)
        tokens = hidden[0, index].astype(jnp.float32)
        masked = tokens * mask[:, None]
        proj = front(masked, w_in_f)
        query = proj[:, :DA]
        keys_low = proj[:, DA : 2 * DA].astype(jnp.bfloat16)
        values_low = proj[:, 2 * DA : 3 * DA].astype(jnp.bfloat16)
        conv_vals = proj[:, 3 * DA :]
        masked_ext, conv_ext = (
            extended_2(masked.astype(jnp.bfloat16), (("seq", 0),), half),
            extended_2(conv_vals.astype(jnp.bfloat16), (("seq", 0),), half),
        )
        masked_ext = masked_ext.astype(jnp.float32)
        conv_ext = conv_ext.astype(jnp.float32)
        key_conv = conv_key(masked_ext, w_depth_f, w_point_f)
        logits = conv_logits(key_conv, query, w_kern_f)
        context_c = conv_mix(logits, conv_ext)
        query_low = query.astype(jnp.bfloat16)
        query_heads = query_low.reshape(length, HEADS, HEAD_DIM)
        top = jnp.full((HEADS, length), neg_fill, jnp.float32)
        key_piece = lax.all_gather(keys_low, "seq", axis=0, tiled=True)
        value_piece = lax.all_gather(values_low, "seq", axis=0, tiled=True)
        count = key_piece.shape[0]
        scores = (
            jnp.einsum(
                "qhd,khd->hqk",
                query_heads,
                key_piece.reshape(count, HEADS, HEAD_DIM),
                preferred_element_type=jnp.float32,
            )
            * scale
        )
        valid = jnp.arange(count, dtype=jnp.int32) < seq_len
        scores = jnp.where(valid[None, None, :], scores, neg_fill)
        new_top = jnp.maximum(top, jnp.max(scores, axis=2))
        probs = jnp.exp(scores - new_top[:, :, None])
        total = jnp.sum(probs, axis=2)
        accum = jnp.einsum(
            "hqk,khd->hqd",
            probs.astype(jnp.bfloat16),
            value_piece.reshape(count, HEADS, HEAD_DIM),
            preferred_element_type=jnp.float32,
        )
        top, total, accum = (new_top, total, accum)
        lse = top + jnp.log(total)
        context_a = (accum / total[:, :, None]).transpose(1, 0, 2).reshape(length, DA)
        context = rounded(jnp.concatenate([context_a, context_c], axis=1))
        branch = end_branch(context, w_out_f)
        first, inner = end_first(branch, tokens, gain_f, bias_f, w_up_f)
        down = end_down(inner, w_down_f)
        result = end_out(first, down, gain_f, bias_f)
        results.append(result.astype(jnp.bfloat16))
        params = widen(
            (
                lax.all_gather(shards[0], ("slot", "seq"), axis=0, tiled=True),
                lax.all_gather(shards[1], ("slot", "seq"), axis=1, tiled=True),
                lax.all_gather(shards[2], ("slot", "seq"), axis=0, tiled=True),
                lax.all_gather(shards[3], ("slot", "seq"), axis=0, tiled=True),
                lax.all_gather(shards[4], ("slot", "seq"), axis=0, tiled=True),
                lax.all_gather(shards[5], ("slot", "seq"), axis=1, tiled=True),
                lax.all_gather(shards[6], ("slot", "seq"), axis=1, tiled=True),
                lax.all_gather(shards[7], ("slot", "seq"), axis=2, tiled=True),
                lax.all_gather(shards[8], ("slot", "seq"), axis=1, tiled=True),
            )
        )
        w_in_f, w_depth_f, w_point_f, w_kern_f, w_out_f, gain_f, bias_f, w_up_f, w_down_f = params
        cotangent = out_grad[0, index].astype(jnp.float32) * mask[:, None]
        _, pull_out = jax.vjp(end_out, first, down, gain_f, bias_f)
        d_first_out, d_down, g_gain_out, g_bias_out = pull_out(cotangent)
        _, pull_down = jax.vjp(end_down, inner, w_down_f)
        d_inner, g_down = pull_down(rounded(d_down))
        _, pull_first = jax.vjp(end_first, branch, tokens, gain_f, bias_f, w_up_f)
        d_branch, d_tokens, g_gain_first, g_bias_first, g_up = pull_first(
            (d_first_out, rounded(d_inner))
        )
        _, pull_branch = jax.vjp(end_branch, context, w_out_f)
        d_context, g_out = pull_branch(rounded(d_branch))
        d_context = rounded(d_context)
        d_ctx_a = d_context[:, :DA]
        d_ctx_c = d_context[:, DA:]
        g_gain = g_gain_out + g_gain_first
        g_bias = g_bias_out + g_bias_first
        key_all, value_all = (
            lax.all_gather(keys_low, "seq", axis=0, tiled=True),
            lax.all_gather(values_low, "seq", axis=0, tiled=True),
        )
        d_query_a, d_keys_all, d_values_all = attend_back(
            query_heads, key_all, value_all, d_ctx_a, context_a, lse, seq_len, scale
        )
        d_keys, d_values = (
            lax.psum_scatter(
                d_keys_all.astype(jnp.bfloat16), "seq", scatter_dimension=0, tiled=True
            ).astype(jnp.float32),
            lax.psum_scatter(
                d_values_all.astype(jnp.bfloat16), "seq", scatter_dimension=0, tiled=True
            ).astype(jnp.float32),
        )
        _, pull_mix = jax.vjp(conv_mix, logits, conv_ext)
        d_logits, d_conv_ext = pull_mix(d_ctx_c)
        _, pull_logits = jax.vjp(conv_logits, key_conv, query, w_kern_f)
        d_key_conv, d_query_c, g_kern = pull_logits(rounded(d_logits))
        _, pull_key = jax.vjp(conv_key, masked_ext, w_depth_f, w_point_f)
        d_masked_ext, g_depth, g_point = pull_key(rounded(d_key_conv))
        send_masked = jnp.concatenate([d_masked_ext[:half], d_masked_ext[-half:]], axis=0)
        send_conv = jnp.concatenate([d_conv_ext[:half], d_conv_ext[-half:]], axis=0)
        back_masked, back_conv = (
            extended_2(send_masked.astype(jnp.bfloat16), (("seq", 0),), half).astype(
                send_masked.dtype
            ),
            extended_2(send_conv.astype(jnp.bfloat16), (("seq", 0),), half).astype(send_conv.dtype),
        )
        d_masked_conv = fold_rims(d_masked_ext, back_masked, half, length)
        d_conv_vals = fold_rims(d_conv_ext, back_conv, half, length)
        _, front_pull = jax.vjp(front, masked, w_in_f)
        d_proj = rounded(
            jnp.concatenate([d_query_a + d_query_c, d_keys, d_values, d_conv_vals], axis=1)
        )
        d_masked, g_in = front_pull(d_proj)
        token_grads.append(
            (d_tokens + (d_masked + d_masked_conv) * mask[:, None]).astype(jnp.bfloat16)
        )
        grads = (g_in, g_depth, g_point, g_kern, g_out, g_gain, g_bias, g_up, g_down)
        if totals is None:
            totals = grads
        else:
            totals = tuple((left_sum + right_sum for left_sum, right_sum in zip(totals, grads)))
    owned = (
        lax.psum_scatter(totals[0], ("slot", "seq"), scatter_dimension=0, tiled=True),
        lax.psum_scatter(totals[1], ("slot", "seq"), scatter_dimension=1, tiled=True),
        lax.psum_scatter(totals[2], ("slot", "seq"), scatter_dimension=0, tiled=True),
        lax.psum_scatter(totals[3], ("slot", "seq"), scatter_dimension=0, tiled=True),
        lax.psum_scatter(totals[4], ("slot", "seq"), scatter_dimension=0, tiled=True),
        lax.psum_scatter(totals[5], ("slot", "seq"), scatter_dimension=1, tiled=True),
        lax.psum_scatter(totals[6], ("slot", "seq"), scatter_dimension=1, tiled=True),
        lax.psum_scatter(totals[7], ("slot", "seq"), scatter_dimension=2, tiled=True),
        lax.psum_scatter(totals[8], ("slot", "seq"), scatter_dimension=1, tiled=True),
    )
    return (
        jnp.stack(results)[None],
        jnp.stack(token_grads)[None],
        owned[0],
        owned[1],
        owned[2],
        owned[3],
        owned[4],
        owned[5],
        owned[6],
        owned[7],
        owned[8],
    )


def solution(mesh):
    placed = (
        P("slot", None, "seq", None),
        P("slot", None, "seq", None),
        P("slot", None),
        P(("slot", "seq"), None),
        P(None, ("slot", "seq")),
        P(("slot", "seq"), None),
        P(("slot", "seq")),
        P(("slot", "seq"), None),
        P(None, ("slot", "seq")),
        P(None, ("slot", "seq")),
        P(None, None, ("slot", "seq")),
        P(None, ("slot", "seq"), None),
    )
    return jax.shard_map(
        per_device,
        mesh=mesh,
        in_specs=placed,
        out_specs=(
            P("slot", None, "seq", None),
            P("slot", None, "seq", None),
            P(("slot", "seq"), None),
            P(None, ("slot", "seq")),
            P(("slot", "seq"), None),
            P(("slot", "seq")),
            P(("slot", "seq"), None),
            P(None, ("slot", "seq")),
            P(None, ("slot", "seq")),
            P(None, None, ("slot", "seq")),
            P(None, ("slot", "seq"), None),
        ),
        check_vma=False,
    )
```

profile of v0, /device:TPU:0, one launch (start us, length us, event | category | flops | bytes accessed | tf_op | source)
XLA Modules:
  0.0 1397.6 jit_solution(5782784756714273040)
XLA Ops:
  10.6 60.2 %all-gather.12.cloned.1.call-done = bf16[768,1536]{1,0:T(8,128)(2,1)} async-done(((bf16[24,1536]{1,0:T(8,128)(2,1)}), bf16[768,1536]{1,0:T(8,128)(2,1)}) %all-gather.12.cloned.1.call-update) | async-done | bytes 2359312 | tf_op jit(solution)/shard_map/all_gather | solution.py:181
  84.4 3.8 collective-permute-start
  92.5 41.9 %all-gather = bf16[32,24,9]{1,2,0:T(8,128)(2,1)S(1)} all-gather(bf16[1,24,9]{1,2,0:T(8,128)(2,1)S(1)} %bitcast.607), channel_id=1, replica_groups=mesh['slot'=2,'seq'=16] {'slot','seq'}, dimensions={0}, use_global_device_ids=true | all-gather | bytes 14256 | tf_op jit(solution)/shard_map/all_gather | solution.py:182
  135.0 38.9 %all_gather.30 = bf16[768,384]{1,0:T(8,128)(2,1)S(1)} all-gather(bf16[24,384]{1,0:T(8,128)(2,1)} %param.21), channel_id=1, replica_groups=mesh['slot'=2,'seq'=16] {'slot','seq'}, dimensions={0}, use_global_device_ids=true | all-gather | bytes 608256 | tf_op jit(solution)/shard_map/all_gather | solution.py:183
  174.0 37.7 %all-gather.1 = bf16[32,24,2]{1,2,0:T(2,128)(2,1)S(1)} all-gather(bf16[1,24,2]{1,2,0:T(2,128)(2,1)S(1)} %bitcast.610), channel_id=1, replica_groups=mesh['slot'=2,'seq'=16] {'slot','seq'}, dimensions={0}, use_global_device_ids=true | all-gather | bytes 3168 | tf_op jit(solution)/shard_map/all_gather | solution.py:186
  212.0 36.8 %all-gather.2 = bf16[32,24,2]{1,2,0:T(2,128)(2,1)S(1)} all-gather(bf16[1,24,2]{1,2,0:T(2,128)(2,1)} %bitcast.611), channel_id=1, replica_groups=mesh['slot'=2,'seq'=16] {'slot','seq'}, dimensions={0}, use_global_device_ids=true | all-gather | bytes 3168 | tf_op jit(solution)/shard_map/all_gather | solution.py:187
  250.5 38.6 %all-reduce.88 = bf16[20736]{0:T(1024)(128)(2,1)S(1)} all-reduce(bf16[20736]{0:T(1024)(128)(2,1)S(1)} %dynamic-update-slice), channel_id=1, replica_groups=mesh['slot'=2,'seq'=16] {'slot','seq'}, use_global_device_ids=true, to_apply=%add.88 | all-reduce | flops 20736 | bytes 82944
  317.3 4.8 collective-permute-start.2
  339.4 4.7 fusion.40
  347.0 5.1 fusion.22
  354.9 4.3 fusion.24
  359.5 2.9 fusion.43
  372.2 39.8 %all-gather.22.cloned.1.call-done = bf16[2,1536,384]{2,1,0:T(8,128)(2,1)} async-done(((bf16[2,48,384]{2,1,0:T(8,128)(2,1)}), bf16[2,1536,384]{2,1,0:T(8,128)(2,1)}) %all-gather.22.cloned.1.call-update) | async-done | bytes 2359312 | tf_op jit(solution)/shard_map/all_gather | solution.py:189
  411.9 3.2 convolution_bitcast_fusion
  429.8 3.5 fusion.52
  443.8 28.8 %while.30 = (s32[]{:T(128)}, f32[128,6,64]{0,2,1:T(8,128)S(1)}, bf16[2,1024,384]{1,2,0:T(8,128)(2,1)}, bf16[2,1024,384]{1,2,0:T(8,128)(2,1)}, s32[2]{0:T(128)S(1...) while((s32[]{:T(128)}, f32[128,6,64]{0,2,1:T(8,128)S(1)}, ...), condition=%wide.region_22.23_spmd.clone, body=%wide.region_21.22_spmd.clone.sunk | while | flops 512116736 | bytes 50344264 | solution.py:155
  485.7 30.2 %while.31 = (s32[]{:T(128)}, f32[128,6,64]{0,2,1:T(8,128)S(1)}, bf16[2,1024,384]{1,2,0:T(8,128)(2,1)}, bf16[2,1024,384]{1,2,0:T(8,128)(2,1)}, s32[2]{0:T(128)}, ...) while((s32[]{:T(128)}, f32[128,6,64]{0,2,1:T(8,128)S(1)}, ...), condition=%wide.region_43.44_spmd.clone, body=%wide.region_42.43_spmd.clone.sunk | while | flops 512116736 | bytes 50737508 | solution.py:155
  554.3 3.2 convolution_add_fusion.1
  559.5 3.1 convolution_add_fusion.2
  571.5 3.9 collective-permute-start.12
  579.8 16.4 %reduce-scatter.17.cloned.1.call-done = bf16[128,384]{1,0:T(8,128)(2,1)} async-done(((bf16[2048,384]{1,0:T(8,128)(2,1)}), bf16[128,384]{1,0:T(8,128)(2,1)}) %reduce-scatter.17.cloned.1.call-update) | async-done | bytes 98320 | tf_op jit(solution)/shard_map/reduce_scatter | solution.py:287
  597.2 61.2 %reduce-scatter.19.cloned.1.call-done = bf16[128,384]{1,0:T(8,128)(2,1)} async-done(((bf16[2048,384]{1,0:T(8,128)(2,1)}), bf16[128,384]{1,0:T(8,128)(2,1)}) %reduce-scatter.19.cloned.1.call-update) | async-done | bytes 98320 | tf_op jit(solution)/shard_map/reduce_scatter | solution.py:284
  658.4 62.5 %reduce-scatter.21.cloned.1.call-done = bf16[128,384]{1,0:T(8,128)(2,1)} async-done(((bf16[2048,384]{1,0:T(8,128)(2,1)}), bf16[128,384]{1,0:T(8,128)(2,1)}) %reduce-scatter.21.cloned.1.call-update) | async-done | bytes 98320 | tf_op jit(solution)/shard_map/reduce_scatter | solution.py:287
  722.8 3.0 convolution_add_fusion
  735.9 43.6 %all-reduce.94 = (f32[9,768]{1,0:T(8,128)S(1)}, f32[2,768]{1,0:T(2,128)S(1)}, f32[2,768]{1,0:T(2,128)}) all-reduce(f32[9,768]{1,0:T(8,128)S(1)} %add_add_fusion.6, f32[2,768]{1,0:T(2,128)S(1)} %add_add_fusion.8, f32[2,768]{1,0:T(2,128)S(1)} %add_add_fusion.7), channel_id=7, replica_groups=mesh['slot'=2,'seq'=16] {'slot','seq'}, use_global_device_ids=true, to_apply=%region_77.78.clone | all-reduce | flops 9984 | bytes 79872
  781.7 3.2 fusion.144
  793.6 51.3 %all-reduce.97.cloned.1.call-done = f32[20736]{0:T(1024)} async-done(((f32[20736]{0:T(1024)}), f32[20736]{0:T(1024)}) %all-reduce.97.cloned.1.call-update) | async-done | bytes 82960
  850.1 98.5 %reduce-scatter.31.cloned.1.call-done = f32[24,384]{1,0:T(8,128)} async-done(((f32[768,384]{1,0:T(8,128)}), f32[24,384]{1,0:T(8,128)}) %reduce-scatter.31.cloned.1.call-update) | async-done | bytes 36880
  948.6 103.8 %reduce-scatter.25.cloned.1.call-done = f32[24,768]{1,0:T(8,128)} async-done(((f32[768,768]{1,0:T(8,128)}), f32[24,768]{1,0:T(8,128)}) %reduce-scatter.25.cloned.1.call-update) | async-done | bytes 73744 | tf_op jit(solution)/shard_map/reduce_scatter | solution.py:325
  1052.4 113.0 %reduce-scatter.29.cloned.1.call-done = f32[2,48,384]{2,1,0:T(8,128)} async-done(((f32[2,1536,384]{2,1,0:T(8,128)}), f32[2,48,384]{2,1,0:T(8,128)}) %reduce-scatter.29.cloned.1.call-update) | async-done | bytes 147472 | tf_op jit(solution)/shard_map/reduce_scatter | solution.py:329
  1165.4 112.0 %reduce-scatter.27.cloned.1.call-done = f32[2,384,48]{1,2,0:T(8,128)} async-done(((f32[2,384,1536]{1,2,0:T(8,128)}), f32[2,384,48]{1,2,0:T(8,128)}) %reduce-scatter.27.cloned.1.call-update) | async-done | bytes 147472 | tf_op jit(solution)/shard_map/reduce_scatter | solution.py:328
  1277.3 113.0 %reduce-scatter.23.cloned.1.call-done = f32[24,1536]{1,0:T(8,128)} async-done(((f32[768,1536]{1,0:T(8,128)}), f32[24,1536]{1,0:T(8,128)}) %reduce-scatter.23.cloned.1.call-update) | async-done | bytes 147472 | tf_op jit(solution)/shard_map/reduce_scatter | solution.py:321
  (951 shorter events, 252.6 us)
Async XLA Ops:
  7.2 63.6 %all-gather.12.cloned.1.call-start = ((), (), s32[]{:S(2)}) async-start(), calls=%async_computation.9 | async-start | bytes 2433024 | tf_op jit(solution)/shard_map/all_gather | solution.py:181
  7.9 319.6 %all-gather.24.cloned.1.call-start = ((), (), s32[]{:S(2)}) async-start(), calls=%async_computation.15 | async-start | bytes 1671168 | tf_op jit(solution)/shard_map/all_gather | solution.py:214
  74.8 261.9 %all-gather.26.cloned.1.call-start = ((), (), s32[]{:S(2)}) async-start(), calls=%async_computation.16 | async-start | bytes 1671168 | tf_op jit(solution)/shard_map/all_gather | solution.py:215
  75.5 268.9 %all-gather.14.cloned.1.call-start = ((), (), s32[]{:S(2)}) async-start(), calls=%async_computation.10 | async-start | bytes 1671168 | tf_op jit(solution)/shard_map/all_gather | solution.py:214
  77.0 275.2 %all-gather.16.cloned.1.call-start = ((), (), s32[]{:S(2)}) async-start(), calls=%async_computation.11 | async-start | bytes 1671168 | tf_op jit(solution)/shard_map/all_gather | solution.py:215
  77.6 285.7 %all-gather.18.cloned.1.call-start = ((), (), s32[]{:S(2)}) async-start(), calls=%async_computation.12 | async-start | bytes 1216512 | tf_op jit(solution)/shard_map/all_gather | solution.py:185
  78.2 289.0 %all-gather.20.cloned.1.call-start = ((), (), s32[]{:S(2)}) async-start(), calls=%async_computation.13 | async-start | bytes 2433024 | tf_op jit(solution)/shard_map/all_gather | solution.py:188
  78.9 333.0 %all-gather.22.cloned.1.call-start = ((), (), s32[]{:S(2)}) async-start(), calls=%async_computation.14 | async-start | bytes 2433024 | tf_op jit(solution)/shard_map/all_gather | solution.py:189
  79.7 210.5 %collective-permute-start.4 = (bf16[4,768]{1,0:T(4,128)(2,1)}, bf16[4,768]{1,0:T(4,128)(2,1)}, u32[]{:S(2)}, u32[]{:S(2)}) collective-permute-start(bf16[4,768]{1,0:T(4,128)(2,1)} %get-tuple-element.562), channel_id=1, source_target_pairs={{0,1},{1,2},{2,3},{3,4},{4,5},{5,6},{6,7},{7,8},{8,9},{9,10},{10,1... | collective-permute-start | bytes 18440 | tf_op jit(solution)/shard_map/ppermute | solution.py:25
  82.5 207.7 %collective-permute-start.5 = (bf16[4,768]{1,0:T(4,128)(2,1)}, bf16[4,768]{1,0:T(4,128)(2,1)}, u32[]{:S(2)}, u32[]{:S(2)}) collective-permute-start(bf16[4,768]{1,0:T(4,128)(2,1)} %get-tuple-element.563), channel_id=1, source_target_pairs={{1,0},{2,1},{3,2},{4,3},{5,4},{6,5},{7,6},{8,7},{9,8},{10,9},{11,1... | collective-permute-start | bytes 18440 | tf_op jit(solution)/shard_map/ppermute | solution.py:28
  84.4 207.4 %collective-permute-start = (bf16[4,768]{1,0:T(4,128)(2,1)}, bf16[4,768]{1,0:T(4,128)(2,1)}, u32[]{:S(2)}, u32[]{:S(2)}) collective-permute-start(bf16[4,768]{1,0:T(4,128)(2,1)} %get-tuple-element.560), channel_id=1, source_target_pairs={{0,1},{1,2},{2,3},{3,4},{4,5},{5,6},{6,7},{7,8},{8,9},{9,10},{10,1... | collective-permute-start | bytes 18440 | tf_op jit(solution)/shard_map/ppermute | solution.py:25
  88.2 203.6 %collective-permute-start.1 = (bf16[4,768]{1,0:T(4,128)(2,1)}, bf16[4,768]{1,0:T(4,128)(2,1)}, u32[]{:S(2)}, u32[]{:S(2)}) collective-permute-start(bf16[4,768]{1,0:T(4,128)(2,1)} %get-tuple-element.561), channel_id=1, source_target_pairs={{1,0},{2,1},{3,2},{4,3},{5,4},{6,5},{7,6},{8,7},{9,8},{10,9},{11,1... | collective-permute-start | bytes 18440 | tf_op jit(solution)/shard_map/ppermute | solution.py:28
  89.5 490.3 %reduce-scatter.15.cloned.1.call-start = ((), (), s32[]{:S(2)}) async-start(), calls=%async_computation.17 | async-start | bytes 1671168 | tf_op jit(solution)/shard_map/reduce_scatter | solution.py:284
  304.2 19.6 %collective-permute-start.6 = (bf16[4,384]{1,0:T(4,128)(2,1)}, bf16[4,384]{1,0:T(4,128)(2,1)}, u32[]{:S(2)}, u32[]{:S(2)}) collective-permute-start(bf16[4,384]{1,0:T(4,128)(2,1)} %get-tuple-element.508), channel_id=1, source_target_pairs={{0,1},{1,2},{2,3},{3,4},{4,5},{5,6},{6,7},{7,8},{8,9},{9,10},{10,1... | collective-permute-start | bytes 9224 | tf_op jit(solution)/shard_map/ppermute | solution.py:25
  306.2 17.7 %collective-permute-start.7 = (bf16[4,384]{1,0:T(4,128)(2,1)}, bf16[4,384]{1,0:T(4,128)(2,1)}, u32[]{:S(2)}, u32[]{:S(2)}) collective-permute-start(bf16[4,384]{1,0:T(4,128)(2,1)} %get-tuple-element.509), channel_id=1, source_target_pairs={{1,0},{2,1},{3,2},{4,3},{5,4},{6,5},{7,6},{8,7},{9,8},{10,9},{11,1... | collective-permute-start | bytes 9224 | tf_op jit(solution)/shard_map/ppermute | solution.py:28
  317.3 8.4 collective-permute-start.2
  475.2 121.0 %reduce-scatter.17.cloned.1.call-start = ((), (), s32[]{:S(2)}) async-start(), calls=%async_computation.18 | async-start | bytes 1671168 | tf_op jit(solution)/shard_map/reduce_scatter | solution.py:287
  482.9 175.5 %reduce-scatter.19.cloned.1.call-start = ((), (), s32[]{:S(2)}) async-start(), calls=%async_computation.19 | async-start | bytes 1671168 | tf_op jit(solution)/shard_map/reduce_scatter | solution.py:284
  518.5 202.4 %reduce-scatter.21.cloned.1.call-start = ((), (), s32[]{:S(2)}) async-start(), calls=%async_computation.20 | async-start | bytes 1671168 | tf_op jit(solution)/shard_map/reduce_scatter | solution.py:287
  538.1 306.9 %all-reduce.97.cloned.1.call-start = ((), (), s32[]{:S(2)}) async-start(), calls=%async_computation.25 | async-start | bytes 172032
  546.2 402.4 %reduce-scatter.31.cloned.1.call-start = ((), (), s32[]{:S(2)}) async-start(), calls=%async_computation.26 | async-start | bytes 1216512
  547.7 504.7 %reduce-scatter.25.cloned.1.call-start = ((), (), s32[]{:S(2)}) async-start(), calls=%async_computation.22 | async-start | bytes 2433024 | tf_op jit(solution)/shard_map/reduce_scatter | solution.py:325
  550.7 614.6 %reduce-scatter.29.cloned.1.call-start = ((), (), s32[]{:S(2)}) async-start(), calls=%async_computation.24 | async-start | bytes 4866048 | tf_op jit(solution)/shard_map/reduce_scatter | solution.py:329
  557.6 719.8 %reduce-scatter.27.cloned.1.call-start = ((), (), s32[]{:S(2)}) async-start(), calls=%async_computation.23 | async-start | bytes 4866048 | tf_op jit(solution)/shard_map/reduce_scatter | solution.py:328
  562.7 827.6 %reduce-scatter.23.cloned.1.call-start = ((), (), s32[]{:S(2)}) async-start(), calls=%async_computation.21 | async-start | bytes 4866048 | tf_op jit(solution)/shard_map/reduce_scatter | solution.py:321
  565.2 11.5 collective-permute-start.8
  567.4 9.3 collective-permute-start.9
  571.5 5.3 collective-permute-start.12
  575.4 4.3 collective-permute-start.13
  732.6 56.1 %collective-permute-start.10 = (bf16[4,768]{1,0:T(4,128)(2,1)S(1)}, bf16[4,768]{1,0:T(4,128)(2,1)}, u32[]{:S(2)}, u32[]{:S(2)}) collective-permute-start(bf16[4,768]{1,0:T(4,128)(2,1)S(1)} %get-tuple-element.510), channel_id=1, source_target_pairs={{0,1},{1,2},{2,3},{3,4},{4,5},{5,6},{6,7},{7,8},{8,9},{9,10},{10,1... | collective-permute-start | bytes 18440 | tf_op jit(solution)/shard_map/ppermute | solution.py:25
  734.5 54.3 %collective-permute-start.11 = (bf16[4,768]{1,0:T(4,128)(2,1)}, bf16[4,768]{1,0:T(4,128)(2,1)}, u32[]{:S(2)}, u32[]{:S(2)}) collective-permute-start(bf16[4,768]{1,0:T(4,128)(2,1)} %get-tuple-element.511), channel_id=1, source_target_pairs={{1,0},{2,1},{3,2},{4,3},{5,4},{6,5},{7,6},{8,7},{9,8},{10,9},{11,1... | collective-permute-start | bytes 18440 | tf_op jit(solution)/shard_map/ppermute | solution.py:28
  787.5 5.5 collective-permute-start.15
  (256 other events, 3813.9 us)
Sparse Core Ops, SparseCore 0:
  10.9 59.8 all-gather.11
  74.9 38.9 all-gather.23
  116.2 38.8 all-gather.25
  157.7 38.8 all-gather.13
  199.4 38.5 all-gather.15
  240.7 52.9 all-gather.17
  296.7 56.0 all-gather.19
  355.7 56.1 all-gather.21
  475.3 58.3 reduce-scatter.14
  537.7 58.4 reduce-scatter.16
  599.9 58.4 reduce-scatter.18
  662.4 58.4 reduce-scatter.20
  726.5 118.4 all-reduce.96
  850.5 98.0 reduce-scatter.30
  954.3 98.0 reduce-scatter.24
  1059.2 106.1 reduce-scatter.28
  1171.3 106.0 reduce-scatter.26
  1284.1 106.1 reduce-scatter.22
where the time goes:
time: 1410 us; the launch traced here: 1400 us
  waiting for transfers between devices  842 us (60%)
  blocking collectives  238 us (17%)
  local copies, waits for them, and re-layouts  123 us (9%)
  matrix products  78.7 us (6%)
  other arithmetic  55.6 us (4%)
  starting transfers between devices  34.1 us (2%)
  between operations  18.7 us (1%)
    unnamed x20, waiting for transfers between devices  153 us
    reduce_scatter x1, waiting for transfers between devices, per_device(): lax.psum_scatter(totals[8], ('slot', 'seq'), scatter_dimension=1, tiled=T...  113 us
    reduce_scatter x1, waiting for transfers between devices, per_device(): lax.psum_scatter(totals[0], ('slot', 'seq'), scatter_dimension=0, tiled=T...  113 us
    reduce_scatter x1, waiting for transfers between devices, per_device(): lax.psum_scatter(totals[7], ('slot', 'seq'), scatter_dimension=2, tiled=T...  112 us
    reduce_scatter x1, waiting for transfers between devices, per_device(): lax.psum_scatter(totals[4], ('slot', 'seq'), scatter_dimension=0, tiled=T...  104 us
    unnamed x2, blocking collectives  82.2 us
    reduce_scatter x2, waiting for transfers between devices, per_device(): lax.psum_scatter(d_values_all.astype(jnp.bfloat16), 'seq', scatter_dimens...  78.9 us
    reduce_scatter x2, waiting for transfers between devices, per_device(): lax.psum_scatter(d_keys_all.astype(jnp.bfloat16), 'seq', scatter_dimensio...  61.2 us
  transfers between devices with their start and end apart: 34, of which 14 were waited for; matrix products, arithmetic and copies ran while one was open for 13% of the time, Pallas kernels for 0%

commit v1 on v0

v1 whole, which is shorter than its diff:
```python
import math

import jax
import jax.numpy as jnp
from jax import lax
from jax.experimental import pallas as pl
from jax.experimental.pallas import tpu as pltpu
from jax.sharding import Mesh, PartitionSpec as P

D = 768
HEADS = 6
HEAD_DIM = 64
KSIZE = 9
GROUPS = 2
DA = 384
HALF = KSIZE // 2

norm_eps = 1e-12
neg_fill = -1e30
bf16 = jnp.bfloat16
f32 = jnp.float32

AXES = ("slot", "grp", "pair", "core")


def swap(value, axis, step):
    count = lax.axis_size(axis)
    return lax.ppermute(value, axis, [(i, i ^ step) for i in range(count)])


def doubled(value, axis):
    count = lax.axis_size(axis)
    value = value[None]
    step = 1
    while step < count:
        value = jnp.concatenate([value, swap(value, axis, step)], axis=0)
        step *= 2
    return value


def halved(value, axis):
    count = lax.axis_size(axis)
    step = count // 2
    while step >= 1:
        got = swap(value[step:], axis, step)
        value = value[:step].astype(f32) + got.astype(f32)
        if step > 1 :
            value = value.astype(bf16)
        step //= 2
    return value[0]


def gather_direct(value, axis):
    count = lax.axis_size(axis)
    return jnp.stack([value] + [swap(value, axis, k) for k in range(1, count)])


def sum_direct(value, axis):
    count = lax.axis_size(axis)
    total = value[0].astype(f32)
    for k in range(1, count):
        total = total + swap(value[k], axis, k).astype(f32)
    return total


def gather_half(piece, order):
    for axis in order:
        piece = doubled(piece, axis)
    return piece


def scatter_half(total, order):
    for axis in reversed(order[1:]):
        total = halved(total, axis).astype(bf16)
    return halved(total, order[0])


ORDER_A = ("grp", "pair", "slot", "core")
ORDER_B = ("grp", "slot", "pair", "core")


def flips(order, to_device):
    axes = AXES if to_device else tuple(reversed(order))
    other = tuple(reversed(order)) if to_device else AXES
    grids = {}
    for d, axis in enumerate(axes):
        shape = [1] * len(axes)
        shape[d] = lax.axis_size(axis)
        grids[axis] = lax.broadcasted_iota(jnp.int32, tuple(shape), d) ^ lax.axis_index(axis)
    idx = jnp.zeros((), jnp.int32)
    for axis in other:
        idx = idx * lax.axis_size(axis) + grids[axis]
    return idx.reshape(-1)


def move_blocks(index, arr, pieces, to_device):
    if to_device:
        n = arr.shape[0]
        out = (pieces, n) + arr.shape[2:]
    else:
        n = arr.shape[1]
        out = (n, pieces) + arr.shape[2:]

    def body(index_ref, src, dst, sem):
        def step(i, carry):
            at = index_ref[i]
            for piece in range(pieces):
                if to_device:
                    pltpu.make_async_copy(src.at[at, piece], dst.at[piece, i], sem).start()
                else:
                    pltpu.make_async_copy(src.at[piece, at], dst.at[i, piece], sem).start()
            return carry

        lax.fori_loop(0, n, step, 0)
        pltpu.make_async_copy(dst, dst, sem).wait()

    return pl.pallas_call(
        body,
        out_shape=jax.ShapeDtypeStruct(out, arr.dtype),
        in_specs=[
            pl.BlockSpec(memory_space=pltpu.SMEM),
            pl.BlockSpec(memory_space=pl.ANY),
        ],
        out_specs=pl.BlockSpec(memory_space=pl.ANY),
        scratch_shapes=[pltpu.SemaphoreType.DMA],
    )(index, arr)


def to_devices(arr, order, pieces):
    flat = arr.reshape((-1,) + arr.shape[-3:])
    moved = move_blocks(flips(order, True), flat, pieces, True)
    return [moved[i].reshape(-1, moved.shape[-1]) for i in range(pieces)]


def from_devices(parts, order, rows):
    arr = jnp.stack([t.astype(bf16).reshape(-1, rows, t.shape[1]) for t in parts])
    return move_blocks(flips(order, False), arr, len(parts), False)


def unflat(arr, order):
    sizes = [lax.axis_size(axis) for axis in reversed(order)]
    return arr.reshape(*sizes, *arr.shape[1:])


def dot(left, right):
    return jnp.dot(left, right, preferred_element_type=f32)


def dot_nt(left, right):
    return lax.dot_general(left, right, (((1,), (1,)), ((), ())), preferred_element_type=f32)


def dot_tn(left, right):
    return lax.dot_general(left, right, (((0,), (0,)), ((), ())), preferred_element_type=f32)


def norm_parts(value):
    centre = value - jnp.mean(value, axis=-1, keepdims=True)
    spread = jnp.mean(centre * centre, axis=-1, keepdims=True)
    inv = lax.rsqrt(spread + norm_eps)
    return centre * inv, inv


def norm_back(hat, inv, grad, gain):
    scaled = grad * gain
    return inv * (
        scaled
        - jnp.mean(scaled, axis=-1, keepdims=True)
        - hat * jnp.mean(scaled * hat, axis=-1, keepdims=True)
    )


def heads_of(value):
    return value.reshape(value.shape[0], HEADS, HEAD_DIM)


def per_device(
    hidden, out_grad, lengths, w_in, w_depth, w_point, w_kern, w_out, ln_gain, ln_bias, w_up, w_down
):
    length = hidden.shape[2]
    groups = lax.axis_size("grp")
    grp, pair, core = (lax.axis_index(a) for a in ("grp", "pair", "core"))
    scale = HEAD_DIM ** (-0.5)
    wide = w_in.shape[0]
    strip = w_kern.shape[0] // wide

    small = jnp.concatenate([w_depth.T, ln_gain.T, ln_bias.T], axis=1)
    small = jnp.pad(small, ((0, 0), (0, 128 - small.shape[1])))
    kern = jnp.pad(w_kern.reshape(wide, strip), ((0, 0), (0, 256 - strip)))
    small = jnp.concatenate([small, kern], axis=1)
    w_q, w_k, w_v, w_c = (w_in[:, i * DA : (i + 1) * DA] for i in range(4))
    early_a = jnp.stack([w_k, w_q, w_point])
    early_b = jnp.stack([w_v, w_c, small])
    fold = w_down.shape[1] // wide
    up_t = w_up.transpose(0, 2, 1).reshape(GROUPS, fold, wide, DA)
    down_r = w_down.reshape(GROUPS, fold, wide, DA)
    late_a = jnp.concatenate([w_out[None, :, :DA], up_t[0], down_r[0]], axis=0)
    late_b = jnp.concatenate([w_out[None, :, DA:], up_t[1], down_r[1]], axis=0)

    tokens2 = jnp.stack([hidden[0], out_grad[0]])
    mine = lax.dynamic_index_in_dim(tokens2, pair, 1, keepdims=False)
    theirs = lax.dynamic_index_in_dim(tokens2, 1 - pair, 1, keepdims=False)
    got = swap(theirs, "pair", 1)
    own_tokens = jnp.stack([mine[0], got[0]])
    own_cot = jnp.stack([mine[1], got[1]]).reshape(2 * length, D).astype(f32)
    full = gather_direct(own_tokens, "grp")
    full = jnp.stack([full, swap(full, "core", 1)])
    seq_len = lax.dynamic_index_in_dim(lengths[0], pair, 0, keepdims=False)

    early_a = gather_half(early_a, ORDER_A)
    early_b = gather_half(early_b, ORDER_B)
    late_a = gather_half(late_a, ORDER_A)
    late_b = gather_half(late_b, ORDER_B)

    def block_id(crel, grel, prel):
        return ((grp ^ grel) * 2 + (pair ^ prel)) * 2 + (core ^ crel)

    crel = jnp.arange(2, dtype=jnp.int32)[:, None, None, None]
    grel = jnp.arange(groups, dtype=jnp.int32)[None, :, None, None]
    prel = jnp.arange(2, dtype=jnp.int32)[None, None, :, None]
    where = block_id(crel, grel, prel) * length + jnp.arange(length, dtype=jnp.int32)
    valid = where < seq_len
    masked = jnp.where(valid[..., None], full, jnp.zeros((), bf16))
    flat_masked = masked.reshape(-1, D)
    total = flat_masked.shape[0]
    blocks = masked.reshape(-1, length, D)
    count = blocks.shape[0]
    own_mask = valid[0, 0].reshape(2 * length).astype(f32)

    def rel_of(block):
        inside = (block >= 0) & (block < count)
        block = jnp.clip(block, 0, count - 1)
        c2, p2, g2 = block % 2, (block // 2) % 2, block // 4
        return ((c2 ^ core) * groups + (g2 ^ grp)) * 2 + (p2 ^ pair), inside

    edges = []
    exts = []
    for b in range(2):
        here = block_id(0, 0, b)
        before, in_b = rel_of(here - 1)
        after, in_a = rel_of(here + 1)
        edges.append((before, in_b, after, in_a))
        head = lax.dynamic_slice(blocks, (before, length - HALF, 0), (1, HALF, D))[0]
        tail = lax.dynamic_slice(blocks, (after, 0, 0), (1, HALF, D))[0]
        exts.append(
            jnp.concatenate(
                [
                    jnp.where(in_b, head, jnp.zeros_like(head)),
                    blocks[b],
                    jnp.where(in_a, tail, jnp.zeros_like(tail)),
                ],
                axis=0,
            )
        )
    ext = jnp.stack(exts)

    mat_k, mat_q, mat_point = to_devices(early_a, ORDER_A, 3)
    mat_v, mat_c, smalls = to_devices(early_b, ORDER_B, 3)
    depth = smalls[:, :KSIZE].T.astype(f32)
    gain = smalls[:, KSIZE : KSIZE + 2].T.astype(f32)
    shift = smalls[:, KSIZE + 2 : KSIZE + 4].T.astype(f32)
    mat_kern = smalls[:, 128 : 128 + strip].reshape(DA, HEADS * KSIZE)
    mat_out = jnp.concatenate(
        to_devices(late_a, ORDER_A, 1) + to_devices(late_b, ORDER_B, 1), axis=1
    )
    mat_up = [t[..., 1 : 1 + fold, :, :].reshape(-1, DA) for t in (late_a, late_b)]
    mat_down = [t[..., 1 + fold :, :, :].reshape(-1, DA) for t in (late_a, late_b)]

    own_masked = blocks[:2].reshape(2 * length, D)
    tokens = own_tokens.reshape(2 * length, D).astype(f32)
    query = dot(own_masked, mat_q).astype(bf16)
    keys = dot(flat_masked, mat_k).astype(bf16)
    values = dot(flat_masked, mat_v).astype(bf16)
    conv_ext = dot(ext.reshape(-1, D), mat_c).astype(bf16).reshape(2, -1, DA)
    ext32 = ext.astype(f32)
    depth_out = sum(depth[j] * ext32[:, j : j + length] for j in range(KSIZE))
    depth_out = depth_out.reshape(2 * length, D).astype(bf16)
    key_conv = dot(depth_out, mat_point)
    query32 = query.astype(f32)
    mixed = (key_conv * query32).astype(bf16)
    logits = dot(mixed, mat_kern).reshape(2 * length, HEADS, KSIZE)
    expo = jnp.exp(logits - jnp.max(logits, axis=-1, keepdims=True))
    kernel = expo / jnp.sum(expo, axis=-1, keepdims=True)
    kernel_wide = [
        jnp.repeat(kernel[:, :, j], HEAD_DIM, axis=1).reshape(2, length, DA) for j in range(KSIZE)
    ]
    conv32 = conv_ext.astype(f32)
    context_c = sum(kernel_wide[j] * conv32[:, j : j + length] for j in range(KSIZE))
    context_c = context_c.reshape(2 * length, DA)

    scores = jnp.einsum("qhd,khd->hqk", heads_of(query), heads_of(keys), preferred_element_type=f32)
    scores = jnp.where(valid.reshape(-1)[None, None, :], scores * scale, neg_fill)
    top = jnp.max(scores, axis=2, keepdims=True)
    probs = jnp.exp(scores - top)
    probs = (probs / jnp.sum(probs, axis=2, keepdims=True)).astype(bf16)
    context_a = jnp.einsum("hqk,khd->qhd", probs, heads_of(values), preferred_element_type=f32)
    context_a = context_a.reshape(2 * length, DA)
    context = jnp.concatenate([context_a, context_c], axis=1).astype(bf16)
    hat1, inv1 = norm_parts(tokens + dot(context, mat_out))
    first = hat1 * gain[0] + shift[0]
    first_low = first.astype(bf16)
    low_g = [first_low[:, :DA], first_low[:, DA:]]
    inner = [dot_nt(low_g[g], mat_up[g]) for g in range(GROUPS)]
    phi = [0.5 * (1.0 + lax.erf(v * 0.7071067811865476)) for v in inner]
    active = [(v * c).astype(bf16) for v, c in zip(inner, phi)]
    down = jnp.concatenate([dot(active[g], mat_down[g]) for g in range(GROUPS)], axis=1)
    hat2, inv2 = norm_parts(first + down)
    result = (hat2 * gain[1] + shift[1]).astype(bf16)

    cot = own_cot * own_mask[:, None]
    g_gain1 = jnp.sum(cot * hat2, axis=0)
    g_bias1 = jnp.sum(cot, axis=0)
    d_r2 = norm_back(hat2, inv2, cot, gain[1])
    d_down = d_r2.astype(bf16)
    d_down_g = [d_down[:, :DA], d_down[:, DA:]]
    g_down = [dot_tn(active[g], d_down_g[g]) for g in range(GROUPS)]
    slope = [
        c + v * jnp.exp(-0.5 * v * v) * 0.3989422804014327 for v, c in zip(inner, phi)
    ]
    d_inner = [(dot_nt(d_down_g[g], mat_down[g]) * slope[g]).astype(bf16) for g in range(GROUPS)]
    g_up = [dot_tn(d_inner[g], low_g[g]) for g in range(GROUPS)]
    d_first = d_r2 + jnp.concatenate([dot(d_inner[g], mat_up[g]) for g in range(GROUPS)], axis=1)
    g_gain0 = jnp.sum(d_first * hat1, axis=0)
    g_bias0 = jnp.sum(d_first, axis=0)
    d_r1 = norm_back(hat1, inv1, d_first, gain[0])
    d_branch = d_r1.astype(bf16)
    g_out = dot_tn(context, d_branch)
    d_context = dot_nt(d_branch, mat_out).astype(bf16)
    d_ctx_a, d_ctx_c = d_context[:, :DA], d_context[:, DA:]

    late_ga = [from_devices([g_out[:, :DA]], ORDER_A, wide)]
    late_gb = [from_devices([g_out[:, DA:]], ORDER_B, wide)]
    for piece in (g_up, g_down):
        late_ga.append(piece[0].astype(bf16).reshape(-1, fold, wide, DA))
        late_gb.append(piece[1].astype(bf16).reshape(-1, fold, wide, DA))
    late_ga = scatter_half(unflat(jnp.concatenate(late_ga, axis=1), ORDER_A), ORDER_A)
    late_gb = scatter_half(unflat(jnp.concatenate(late_gb, axis=1), ORDER_B), ORDER_B)

    p32 = probs.astype(f32)
    d_heads = heads_of(d_ctx_a)
    d_values = jnp.einsum("hqk,qhd->khd", probs, d_heads, preferred_element_type=f32)
    d_probs = jnp.einsum("qhd,khd->hqk", d_heads, heads_of(values), preferred_element_type=f32)
    delta = jnp.sum(p32 * d_probs, axis=2, keepdims=True)
    d_scores = (p32 * (d_probs - delta)).astype(bf16)
    d_query_a = jnp.einsum("hqk,khd->qhd", d_scores, heads_of(keys), preferred_element_type=f32)
    d_query_a = d_query_a.reshape(2 * length, DA) * scale
    d_keys = jnp.einsum("hqk,qhd->khd", d_scores, heads_of(query), preferred_element_type=f32)
    d_keys = (d_keys.reshape(-1, DA) * scale).astype(bf16)
    d_values = d_values.reshape(-1, DA).astype(bf16)

    d_ctx_c32 = d_ctx_c.astype(f32).reshape(2, length, DA)
    d_kernel = jnp.stack(
        [
            jnp.sum(
                (d_ctx_c32 * conv32[:, j : j + length]).reshape(2 * length, HEADS, HEAD_DIM), axis=2
            )
            for j in range(KSIZE)
        ],
        axis=2,
    )
    d_conv_ext = sum(
        jnp.pad(kernel_wide[j] * d_ctx_c32, ((0, 0), (j, KSIZE - 1 - j), (0, 0)))
        for j in range(KSIZE)
    )
    d_conv_ext = d_conv_ext.astype(bf16).reshape(-1, DA)
    d_logits = kernel * (d_kernel - jnp.sum(kernel * d_kernel, axis=2, keepdims=True))
    d_logits = d_logits.astype(bf16).reshape(2 * length, HEADS * KSIZE)
    g_kern = dot_tn(mixed, d_logits)
    d_mixed = dot_nt(d_logits, mat_kern)
    d_key_conv = (d_mixed * query32).astype(bf16)
    d_query = (d_query_a + d_mixed * key_conv).astype(bf16)
    g_point = dot_tn(depth_out, d_key_conv)
    d_depth = dot_nt(d_key_conv, mat_point).reshape(2, length, D)
    g_depth = jnp.stack(
        [jnp.sum(d_depth * ext32[:, j : j + length], axis=(0, 1)) for j in range(KSIZE)], axis=1
    )
    d_ext = sum(
        jnp.pad(depth[j] * d_depth, ((0, 0), (j, KSIZE - 1 - j), (0, 0))) for j in range(KSIZE)
    )
    d_ext = d_ext + dot_nt(d_conv_ext, mat_c).reshape(2, -1, D)

    d_full = dot_nt(d_keys, mat_k) + dot_nt(d_values, mat_v)
    d_full = d_full.reshape(count, length, D)
    d_own = d_ext[:, HALF : HALF + length] + dot_nt(d_query, mat_q).reshape(2, length, D)
    d_full = jnp.concatenate([d_full[:2] + d_own, d_full[2:]], axis=0)
    for b in range(2):
        before, in_b, after, in_a = edges[b]
        for place, row, rows, inside in (
            (before, length - HALF, d_ext[b, :HALF], in_b),
            (after, 0, d_ext[b, -HALF:], in_a),
        ):
            old = lax.dynamic_slice(d_full, (place, row, 0), (1, HALF, D))
            new = old + jnp.where(inside, rows, 0.0)[None]
            d_full = lax.dynamic_update_slice(d_full, new, (place, row, 0))
    d_full = d_full.astype(bf16).reshape(2, groups, 2, length, D)
    d_full = d_full[0].astype(f32) + swap(d_full[1], "core", 1).astype(f32)
    d_full = sum_direct(d_full.astype(bf16), "grp")
    d_hidden = d_r1 + d_full.reshape(2 * length, D) * own_mask[:, None]
    d_hidden = d_hidden.astype(bf16)

    g_q = dot_tn(own_masked, d_query)
    g_k = dot_tn(flat_masked, d_keys)
    g_v = dot_tn(flat_masked, d_values)
    g_c = dot_tn(ext.reshape(-1, D), d_conv_ext)
    g_small = jnp.concatenate(
        [g_depth, g_gain0[:, None], g_gain1[:, None], g_bias0[:, None], g_bias1[:, None]], axis=1
    )
    g_small = jnp.pad(g_small, ((0, 0), (0, 128 - g_small.shape[1])))
    g_kern = jnp.pad(g_kern.reshape(D, strip), ((0, 0), (0, 256 - strip)))
    g_small = jnp.concatenate([g_small, g_kern], axis=1)
    early_ga = from_devices([g_k, g_q, g_point], ORDER_A, wide)
    early_gb = from_devices([g_v, g_c, g_small], ORDER_B, wide)
    early_ga = scatter_half(unflat(early_ga, ORDER_A), ORDER_A)
    early_gb = scatter_half(unflat(early_gb, ORDER_B), ORDER_B)

    outs = jnp.stack([result, d_hidden]).reshape(2, 2, length, D)
    got = swap(outs[:, 1], "pair", 1)
    kept = outs[:, 0]
    final = jnp.where(
        pair == 0, jnp.stack([kept, got], axis=1), jnp.stack([got, kept], axis=1)
    )
    g_small = early_gb[2]
    late = [late_ga, late_gb]
    return (
        final[0][None],
        final[1][None],
        jnp.concatenate([early_ga[1], early_ga[0], early_gb[0], early_gb[1]], axis=1),
        g_small[:, :KSIZE].T,
        early_ga[2],
        g_small[:, 128 : 128 + strip].reshape(-1),
        jnp.concatenate([late_ga[0], late_gb[0]], axis=1),
        g_small[:, KSIZE : KSIZE + 2].T,
        g_small[:, KSIZE + 2 : KSIZE + 4].T,
        jnp.stack([t[1 : 1 + fold].reshape(-1, DA).T for t in late]),
        jnp.stack([t[1 + fold :].reshape(-1, DA) for t in late]),
    )


def solution(mesh):
    slots, places = mesh.shape["slot"], mesh.shape["seq"]
    fine = Mesh(mesh.devices.reshape(slots, places // 4, 2, 2), AXES)
    seq = AXES[1:]
    placed = (
        P("slot", None, seq, None),
        P("slot", None, seq, None),
        P("slot", None),
        P(AXES, None),
        P(None, AXES),
        P(AXES, None),
        P(AXES),
        P(AXES, None),
        P(None, AXES),
        P(None, AXES),
        P(None, None, AXES),
        P(None, AXES, None),
    )
    return jax.shard_map(
        per_device,
        mesh=fine,
        in_specs=placed,
        out_specs=(placed[0], placed[1]) + placed[3:],
        check_vma=False,
    )
```

time: 1410 us -> 764 us (0.54)
  waiting for transfers between devices: 842 us -> 112 us
  Pallas kernels: 0 us -> 301 us
  blocking collectives: 238 us -> 0 us
  other arithmetic: 55.6 us -> 104 us
  starting transfers between devices: 34.1 us -> 55.9 us
  between operations: 18.7 us -> 3.67 us
  local copies, waits for them, and re-layouts: 123 us -> 108 us
    reduce_scatter x8 -> x0, waiting for transfers between devices: 582 us -> none  [the longest x1 113 us: per_device(): lax.psum_scatter(totals[8], ('slot', 'seq'), scatter_dimension=1, tiled=T...]
    pallas_call x0 -> x8, Pallas kernels: none -> 301 us  [move_blocks(): pl.pallas_call(body, out_shape=jax.ShapeDtypeStruct(out, arr.dtype), in_s...]
    all_gather x4 -> x0, blocking collectives: 155 us -> none  [the longest x1 41.9 us: per_device(): lax.all_gather(shards[1], ('slot', 'seq'), axis=1, tiled=True)]
    unnamed x20 -> x0, waiting for transfers between devices: 153 us -> none
    ppermute x16 -> x50, waiting for transfers between devices: 6.56 us -> 112 us  [swap(): return lax.ppermute(value, axis, [(i, i ^ step) for i in range(count)])]
    all_gather x8 -> x0, waiting for transfers between devices: 100 us -> none  [the longest x1 60.2 us: per_device(): lax.all_gather(shards[0], ('slot', 'seq'), axis=0, tiled=True)]
    unnamed x2 -> x0, blocking collectives: 82.2 us -> none
    convert_element_type x19 -> x28, other arithmetic: 9.71 us -> 37.2 us  [the longest x1 9.4 us: per_device(): probs = (probs / jnp.sum(probs, axis=2, keepdims=True)).astype(bf16)]
  transfers between devices with their start and end apart: 34 -> 50, of which waited for: 14 -> 17; matrix products, arithmetic and copies ran while one was open for 13% -> 23% of each run, Pallas kernels for 0% -> 32%
where the time goes in v1:
time: 764 us; the launch traced here: 755 us
  Pallas kernels  301 us (39%)
  waiting for transfers between devices  112 us (15%)
  local copies, waits for them, and re-layouts  108 us (14%)
  other arithmetic  104 us (14%)
  matrix products  70.8 us (9%)
  starting transfers between devices  55.9 us (7%)
    pallas_call x8, Pallas kernels, move_blocks(): pl.pallas_call(body, out_shape=jax.ShapeDtypeStruct(out, arr.dtype), in_s...  301 us
    ppermute x50, waiting for transfers between devices, swap(): return lax.ppermute(value, axis, [(i, i ^ step) for i in range(count)])  112 us
    ppermute x50, starting transfers between devices, swap(): return lax.ppermute(value, axis, [(i, i ^ step) for i in range(count)])  55.9 us
    unnamed x275, local copies, waits for them, and re-layouts  35.7 us
    dot_general x11, matrix products, dot_nt(): lax.dot_general(left, right, (((1,), (1,)), ((), ())), preferred_element_...  18.4 us
    dot_general x11, matrix products, dot_tn(): lax.dot_general(left, right, (((0,), (0,)), ((), ())), preferred_element_...  17 us
    concatenate x10, other arithmetic, doubled(): value = jnp.concatenate([value, swap(value, axis, step)], axis=0)  16.4 us
  transfers between devices with their start and end apart: 50, of which 17 were waited for; matrix products, arithmetic and copies ran while one was open for 23% of the time, Pallas kernels for 32%

profile of v1, /device:TPU:0, one launch (start us, length us, event | category | flops | bytes accessed | tf_op | source)
XLA Modules:
  0.0 754.6 jit_solution(2562051069778723364)
XLA Ops:
  23.6 14.5 %collective-permute-done.11 = bf16[2,3,24,384]{3,2,1,0:T(8,128)(2,1)S(1)} collective-permute-done((bf16[2,3,24,384]{3,2,1,0:T(8,128)(2,1)S(1)}, bf16[2,3,24,384]{3,2,1,0:T(8,128)(2,1)S(1)}, u32[]{:S(2)}, u32[]{:S(2)}) %collective-permute-start.11) | collective-permute-done | bytes 110624 | tf_op jit(solution)/shard_map/ppermute | solution.py:28
  40.4 4.3 collective-permute-done.16
  51.3 5.1 collective-permute-done.17
  57.1 3.4 collective-permute-start.3
  65.3 14.8 %collective-permute-done.2 = bf16[2,128,768]{2,1,0:T(8,128)(2,1)S(1)} collective-permute-done((bf16[2,128,768]{2,1,0:T(8,128)(2,1)}, bf16[2,128,768]{2,1,0:T(8,128)(2,1)S(1)}, u32[]{:S(2)}, u32[]{:S(2)}) %collective-permute-start.2) | collective-permute-done | bytes 393248 | tf_op jit(solution)/shard_map/ppermute | solution.py:28
  100.3 55.4 %shard_map.203 = bf16[3,32,24,384]{3,2,1,0:T(8,128)(2,1)} custom-call(s32[32]{0:T(128)} %add.777.index_ref, bf16[32,3,24,384]{3,2,1,0:T(8,128)(2,1)} %bitcast.554), custom_call_target="tpu_custom_call" | custom-call | tf_op jit(solution)/shard_map/pallas_call | solution.py:117
  174.5 55.5 %shard_map.204 = bf16[3,32,24,384]{3,2,1,0:T(8,128)(2,1)} custom-call(s32[32]{0:T(128)} %add.788.index_ref, bf16[32,3,24,384]{3,2,1,0:T(8,128)(2,1)} %bitcast.555), custom_call_target="tpu_custom_call" | custom-call | tf_op jit(solution)/shard_map/pallas_call | solution.py:117
  282.2 4.5 convolution_convert_fusion.1
  286.7 9.8 %fusion.123 = (f32[6,256]{1,0:T(8,128)S(1)}, f32[6,256,2048]{2,1,0:T(8,128)}) fusion(pred[2048]{0:T(1024)(128)(4,1)S(1)} %copy-done.117, bf16[256,6,64]{0,2,1:T(8,128)(2,1)} %bitcast.644, bf16[2048,6,64]{0,2,1:T(8,128)(2,1)} %bitcast.623), kind=kOutput, calls=%fused_computation.403 | convolution fusion | flops 415238144 | bytes 14360576 | tf_op jit(solution)/shard_map/sub | solution.py:294
  296.5 9.4 %divide_convert_fusion = bf16[6,256,2048]{2,1,0:T(8,128)(2,1)} fusion(f32[6,256,2048]{2,1,0:T(8,128)} %get-tuple-element.202, f32[6,256]{1,0:T(8,128)S(1)} %get-tuple-element.201), kind=kLoop, calls=%fused_computation.7 | loop fusion | flops 6291456 | bytes 18880512 | tf_op jit(solution)/shard_map/convert_element_type | solution.py:295
  306.0 4.1 add_convert_fusion.4
  315.6 3.9 pad_maximum_fusion.2
  319.5 19.6 %shard_map.206 = bf16[1,32,24,384]{3,2,1,0:T(8,128)(2,1)} custom-call(s32[32]{0:T(128)} %add.777.index_ref, bf16[32,5,24,384]{3,2,1,0:T(8,128)(2,1)} %bitcast.548), custom_call_target="tpu_custom_call" | custom-call | tf_op jit(solution)/shard_map/pallas_call | solution.py:117
  342.5 19.6 %shard_map.205 = bf16[1,32,24,384]{3,2,1,0:T(8,128)(2,1)} custom-call(s32[32]{0:T(128)} %add.788.index_ref, bf16[32,5,24,384]{3,2,1,0:T(8,128)(2,1)} %bitcast.549), custom_call_target="tpu_custom_call" | custom-call | tf_op jit(solution)/shard_map/pallas_call | solution.py:117
  391.4 4.2 convolution_convert_fusion
  398.0 6.2 fusion.4
  426.1 5.5 fusion.113
  439.0 8.2 %add_convert_fusion = bf16[2,136,384]{1,0,2:T(2,128)(2,1)S(1)} fusion(f32[2,128,384]{1,0,2:T(2,128)S(1)} %bitcast.636, f32[2,128,384]{1,0,2:T(2,128)} %bitcast.637, f32[2,128,384]{1,0,2:T(2,128)} %bitcast.638, f32[2,128,384]{1,0,2:T(2,128)} %bitcast.639, f32[2,128,384]{1,0,2:T(2,128)} %bitcast.640, f32[2,128,384]{1,0,2:T(2,128)} %bitcast.641, ...), kind=kLoop, calls=%fused_computation.136 | loop fusion | flops 940032 | bytes 3747840 | tf_op jit(solution)/shard_map/convert_element_type | solution.py:365
  451.6 19.8 %shard_map.210 = bf16[32,1,24,384]{3,2,1,0:T(8,128)(2,1)} custom-call(s32[32]{0:T(128)} %add.896.index_ref, bf16[1,32,24,384]{3,2,1,0:T(8,128)(2,1)} %bitcast.615), custom_call_target="tpu_custom_call" | custom-call | tf_op jit(solution)/shard_map/pallas_call | solution.py:117
  474.6 19.6 %shard_map.209 = bf16[32,1,24,384]{3,2,1,0:T(8,128)(2,1)} custom-call(s32[32]{0:T(128)} %add.885.index_ref, bf16[1,32,24,384]{3,2,1,0:T(8,128)(2,1)} %bitcast.614), custom_call_target="tpu_custom_call" | custom-call | tf_op jit(solution)/shard_map/pallas_call | solution.py:117
  504.5 55.4 %shard_map.207 = bf16[32,3,24,384]{3,2,1,0:T(8,128)(2,1)} custom-call(s32[32]{0:T(128)} %add.885.index_ref, bf16[3,32,24,384]{3,2,1,0:T(8,128)(2,1)} %pad_maximum_fusion.8.src), custom_call_target="tpu_custom_call" | custom-call | tf_op jit(solution)/shard_map/pallas_call | solution.py:117
  563.5 4.4 multiply_reduce_fusion.2
  570.6 55.5 %shard_map.208 = bf16[32,3,24,384]{3,2,1,0:T(8,128)(2,1)} custom-call(s32[32]{0:T(128)} %add.896.index_ref, bf16[3,32,24,384]{3,2,1,0:T(8,128)(2,1)} %maximum_maximum_fusion.src), custom_call_target="tpu_custom_call" | custom-call | tf_op jit(solution)/shard_map/pallas_call | solution.py:117
  628.1 3.7 convolution_add_fusion.1
  637.7 10.9 %collective-permute-done.31 = bf16[1,2,4,3,24,384]{5,4,3,2,1,0:T(8,128)(2,1)S(1)} collective-permute-done((bf16[1,2,4,3,24,384]{5,4,3,2,1,0:T(8,128)(2,1)S(1)}, bf16[1,2,4,3,24,384]{5,4,3,2,1,0:T(8,128)(2,1)S(1)}, u32[]{:S(2)}, u32[]{:S(2)}) %collective-permute-start.31) | collective-permute-done | bytes 442400 | tf_op jit(solution)/shard_map/ppermute | solution.py:28
  665.0 3.8 collective-permute-done.33
  671.4 11.9 %collective-permute-done.34 = bf16[1,3,24,384]{3,2,1,0:T(8,128)(2,1)S(1)} collective-permute-done((bf16[1,3,24,384]{3,2,1,0:T(8,128)(2,1)S(1)}, bf16[1,3,24,384]{3,2,1,0:T(8,128)(2,1)S(1)}, u32[]{:S(2)}, u32[]{:S(2)}) %collective-permute-start.34) | collective-permute-done | bytes 55328 | tf_op jit(solution)/shard_map/ppermute | solution.py:28
  687.5 6.0 collective-permute-start.27
  696.9 13.0 %collective-permute-done.27 = bf16[2,128,768]{2,1,0:T(8,128)(2,1)} collective-permute-done((bf16[2,128,768]{2,1,0:T(8,128)(2,1)}, bf16[2,128,768]{2,1,0:T(8,128)(2,1)}, u32[]{:S(2)}, u32[]{:S(2)}) %collective-permute-start.27) | collective-permute-done | bytes 393248 | tf_op jit(solution)/shard_map/ppermute | solution.py:28
  717.6 6.7 collective-permute-done.29
  725.4 4.6 collective-permute-done.42
  733.3 12.1 %collective-permute-done.43 = bf16[2,5,24,384]{3,2,1,0:T(8,128)(2,1)S(1)} collective-permute-done((bf16[2,5,24,384]{3,2,1,0:T(8,128)(2,1)S(1)}, bf16[2,5,24,384]{3,2,1,0:T(8,128)(2,1)S(1)}, u32[]{:S(2)}, u32[]{:S(2)}) %collective-permute-start.43) | collective-permute-done | bytes 184352 | tf_op jit(solution)/shard_map/ppermute | solution.py:28
  (647 shorter events, 275.2 us)
Async XLA Ops:
  3.1 14.3 %collective-permute-start.5 = (bf16[1,3,24,384]{3,2,1,0:T(8,128)(2,1)S(1)}, bf16[1,3,24,384]{3,2,1,0:T(8,128)(2,1)S(1)}, u32[]{:S(2)}, u32[]{:S(2)}) collective-permute-start(bf16[1,3,24,384]{3,2,1,0:T(8,128)(2,1)S(1)} %maximum_bitcast_fusion.16), channel_id=1, source_target_pairs={{0,4},{4,0},{8,12},{12,8},{1,5},{5,1},{9,13},{13,9},{2,6},{6,2},{1... | collective-permute-start | bytes 165896 | tf_op jit(solution)/shard_map/ppermute | solution.py:28
  7.0 13.1 %collective-permute-start.10 = (bf16[1,3,24,384]{3,2,1,0:T(8,128)(2,1)S(1)}, bf16[1,3,24,384]{3,2,1,0:T(8,128)(2,1)S(1)}, u32[]{:S(2)}, u32[]{:S(2)}) collective-permute-start(bf16[1,3,24,384]{3,2,1,0:T(8,128)(2,1)S(1)} %maximum_bitcast_fusion.17), channel_id=1, source_target_pairs={{0,4},{4,0},{8,12},{12,8},{1,5},{5,1},{9,13},{13,9},{2,6},{6,2},{1... | collective-permute-start | bytes 165896 | tf_op jit(solution)/shard_map/ppermute | solution.py:28
  13.4 35.8 %collective-permute-start = (bf16[2,128,768]{2,1,0:T(8,128)(2,1)}, bf16[2,128,768]{2,1,0:T(8,128)(2,1)}, u32[]{:S(2)}, u32[]{:S(2)}) collective-permute-start(bf16[2,128,768]{2,1,0:T(8,128)(2,1)} %dynamic-slice_bitcast_fusion), channel_id=1, source_target_pairs={{0,2},{2,0},{1,3},{3,1},{4,6},{6,4},{5,7},{7,5},{8,10},{10,8},{9,1... | collective-permute-start | bytes 1179656 | tf_op jit(solution)/shard_map/ppermute | solution.py:28
  17.4 21.1 %collective-permute-start.6 = (bf16[2,3,24,384]{3,2,1,0:T(8,128)(2,1)S(1)}, bf16[2,3,24,384]{3,2,1,0:T(8,128)(2,1)S(1)}, u32[]{:S(2)}, u32[]{:S(2)}) collective-permute-start(bf16[2,3,24,384]{3,2,1,0:T(8,128)(2,1)S(1)} %pad_maximum_fusion.27), channel_id=1, source_target_pairs={{0,8},{4,12},{8,0},{12,4},{1,9},{5,13},{9,1},{13,5},{2,10},{6,14},... | collective-permute-start | bytes 331784 | tf_op jit(solution)/shard_map/ppermute | solution.py:28
  20.1 18.0 %collective-permute-start.11 = (bf16[2,3,24,384]{3,2,1,0:T(8,128)(2,1)S(1)}, bf16[2,3,24,384]{3,2,1,0:T(8,128)(2,1)S(1)}, u32[]{:S(2)}, u32[]{:S(2)}) collective-permute-start(bf16[2,3,24,384]{3,2,1,0:T(8,128)(2,1)S(1)} %pad_maximum_fusion.28), channel_id=1, source_target_pairs={{0,8},{4,12},{8,0},{12,4},{1,9},{5,13},{9,1},{13,5},{2,10},{6,14},... | collective-permute-start | bytes 331784 | tf_op jit(solution)/shard_map/ppermute | solution.py:28
  20.5 24.8 %collective-permute-start.21 = (bf16[2,5,24,384]{3,2,1,0:T(8,128)(2,1)S(1)}, bf16[2,5,24,384]{3,2,1,0:T(8,128)(2,1)S(1)}, u32[]{:S(2)}, u32[]{:S(2)}) collective-permute-start(bf16[2,5,24,384]{3,2,1,0:T(8,128)(2,1)S(1)} %pad_maximum_fusion.23), channel_id=1, source_target_pairs={{0,8},{4,12},{8,0},{12,4},{1,9},{5,13},{9,1},{13,5},{2,10},{6,14},... | collective-permute-start | bytes 552968 | tf_op jit(solution)/shard_map/ppermute | solution.py:28
  23.2 21.5 %collective-permute-start.16 = (bf16[2,5,24,384]{3,2,1,0:T(8,128)(2,1)S(1)}, bf16[2,5,24,384]{3,2,1,0:T(8,128)(2,1)S(1)}, u32[]{:S(2)}, u32[]{:S(2)}) collective-permute-start(bf16[2,5,24,384]{3,2,1,0:T(8,128)(2,1)S(1)} %pad_maximum_fusion.22), channel_id=1, source_target_pairs={{0,8},{4,12},{8,0},{12,4},{1,9},{5,13},{9,1},{13,5},{2,10},{6,14},... | collective-permute-start | bytes 552968 | tf_op jit(solution)/shard_map/ppermute | solution.py:28
  47.1 16.5 %collective-permute-start.8 = (bf16[1,2,4,3,24,384]{5,4,3,2,1,0:T(8,128)(2,1)S(1)}, bf16[1,2,4,3,24,384]{5,4,3,2,1,0:T(8,128)(2,1)S(1)}, u32[]{:S(2)}, u32[]{:S(2)}) collective-permute-start(bf16[1,2,4,3,24,384]{5,4,3,2,1,0:T(8,128)(2,1)S(1)} %maximum_bitcast_fusion.6), channel_id=1, source_target_pairs={{0,2},{2,0},{1,3},{3,1},{4,6},{6,4},{5,7},{7,5},{8,10},{10,8},{9,1... | collective-permute-start | bytes 1327112 | tf_op jit(solution)/shard_map/ppermute | solution.py:28
  48.7 42.1 %collective-permute-start.13 = (bf16[1,2,4,3,24,384]{5,4,3,2,1,0:T(8,128)(2,1)S(1)}, bf16[1,2,4,3,24,384]{5,4,3,2,1,0:T(8,128)(2,1)}, u32[]{:S(2)}, u32[]{:S(2)}) collective-permute-start(bf16[1,2,4,3,24,384]{5,4,3,2,1,0:T(8,128)(2,1)S(1)} %maximum_bitcast_fusion.7), channel_id=1, source_target_pairs={{0,16},{16,0},{1,17},{17,1},{2,18},{18,2},{3,19},{19,3},{4,20},{20... | collective-permute-start | bytes 1327112 | tf_op jit(solution)/shard_map/ppermute | solution.py:28
  51.3 28.8 %collective-permute-start.2 = (bf16[2,128,768]{2,1,0:T(8,128)(2,1)}, bf16[2,128,768]{2,1,0:T(8,128)(2,1)S(1)}, u32[]{:S(2)}, u32[]{:S(2)}) collective-permute-start(bf16[2,128,768]{2,1,0:T(8,128)(2,1)} %get-tuple-element.148), channel_id=1, source_target_pairs={{0,8},{4,12},{8,0},{12,4},{1,9},{5,13},{9,1},{13,5},{2,10},{6,14},... | collective-permute-start | bytes 1179656 | tf_op jit(solution)/shard_map/ppermute | solution.py:28
  56.4 25.3 %collective-permute-start.1 = (bf16[2,128,768]{2,1,0:T(8,128)(2,1)}, bf16[2,128,768]{2,1,0:T(8,128)(2,1)S(1)}, u32[]{:S(2)}, u32[]{:S(2)}) collective-permute-start(bf16[2,128,768]{2,1,0:T(8,128)(2,1)} %get-tuple-element.148), channel_id=1, source_target_pairs={{0,4},{4,0},{8,12},{12,8},{1,5},{5,1},{9,13},{13,9},{2,6},{6,2},{1... | collective-permute-start | bytes 1179656 | tf_op jit(solution)/shard_map/ppermute | solution.py:28
  57.1 30.4 %collective-permute-start.3 = (bf16[2,128,768]{2,1,0:T(8,128)(2,1)}, bf16[2,128,768]{2,1,0:T(8,128)(2,1)}, u32[]{:S(2)}, u32[]{:S(2)}) collective-permute-start(bf16[2,128,768]{2,1,0:T(8,128)(2,1)} %get-tuple-element.148), channel_id=1, source_target_pairs={{0,12},{4,8},{8,4},{12,0},{1,13},{5,9},{9,5},{13,1},{2,14},{6,10},... | collective-permute-start | bytes 1179656 | tf_op jit(solution)/shard_map/ppermute | solution.py:28
  63.6 31.1 %collective-permute-start.23 = (bf16[1,2,4,5,24,384]{5,4,3,2,1,0:T(8,128)(2,1)}, bf16[1,2,4,5,24,384]{5,4,3,2,1,0:T(8,128)(2,1)}, u32[]{:S(2)}, u32[]{:S(2)}) collective-permute-start(bf16[1,2,4,5,24,384]{5,4,3,2,1,0:T(8,128)(2,1)} %maximum_bitcast_fusion.5), channel_id=1, source_target_pairs={{0,2},{2,0},{1,3},{3,1},{4,6},{6,4},{5,7},{7,5},{8,10},{10,8},{9,1... | collective-permute-start | bytes 2211848 | tf_op jit(solution)/shard_map/ppermute | solution.py:28
  80.1 12.9 %collective-permute-start.18 = (bf16[1,2,4,5,24,384]{5,4,3,2,1,0:T(8,128)(2,1)S(1)}, bf16[1,2,4,5,24,384]{5,4,3,2,1,0:T(8,128)(2,1)}, u32[]{:S(2)}, u32[]{:S(2)}) collective-permute-start(bf16[1,2,4,5,24,384]{5,4,3,2,1,0:T(8,128)(2,1)S(1)} %maximum_bitcast_fusion.4), channel_id=1, source_target_pairs={{0,16},{16,0},{1,17},{17,1},{2,18},{18,2},{3,19},{19,3},{4,20},{20... | collective-permute-start | bytes 2211848 | tf_op jit(solution)/shard_map/ppermute | solution.py:28
  82.4 15.1 %collective-permute-start.9 = (bf16[1,2,2,4,3,24,384]{6,5,4,3,2,1,0:T(8,128)(2,1)}, bf16[1,2,2,4,3,24,384]{6,5,4,3,2,1,0:T(8,128)(2,1)}, u32[]{:S(2)}, u32[]{:S(2)}) collective-permute-start(bf16[1,2,2,4,3,24,384]{6,5,4,3,2,1,0:T(8,128)(2,1)} %maximum_bitcast_fusion.2), channel_id=1, source_target_pairs={{0,1},{1,0},{2,3},{3,2},{4,5},{5,4},{6,7},{7,6},{8,9},{9,8},{10,11... | collective-permute-start | bytes 2654216 | tf_op jit(solution)/shard_map/ppermute | solution.py:28
  90.3 145.0 %collective-permute-start.4 = (bf16[4,2,128,768]{3,2,1,0:T(8,128)(2,1)}, bf16[4,2,128,768]{3,2,1,0:T(8,128)(2,1)}, u32[]{:S(2)}, u32[]{:S(2)}) collective-permute-start(bf16[4,2,128,768]{3,2,1,0:T(8,128)(2,1)} %get-tuple-element.100), channel_id=1, source_target_pairs={{0,1},{1,0},{2,3},{3,2},{4,5},{5,4},{6,7},{7,6},{8,9},{9,8},{10,11... | collective-permute-start | bytes 4718600 | tf_op jit(solution)/shard_map/ppermute | solution.py:28
  92.9 78.7 %collective-permute-start.14 = (bf16[1,2,2,4,3,24,384]{6,5,4,3,2,1,0:T(8,128)(2,1)}, bf16[1,2,2,4,3,24,384]{6,5,4,3,2,1,0:T(8,128)(2,1)}, u32[]{:S(2)}, u32[]{:S(2)}) collective-permute-start(bf16[1,2,2,4,3,24,384]{6,5,4,3,2,1,0:T(8,128)(2,1)} %maximum_bitcast_fusion.3), channel_id=1, source_target_pairs={{0,1},{1,0},{2,3},{3,2},{4,5},{5,4},{6,7},{7,6},{8,9},{9,8},{10,11... | collective-permute-start | bytes 2654216 | tf_op jit(solution)/shard_map/ppermute | solution.py:28
  94.3 244.9 %collective-permute-start.19 = (bf16[1,2,2,4,5,24,384]{6,5,4,3,2,1,0:T(8,128)(2,1)S(1)}, bf16[1,2,2,4,5,24,384]{6,5,4,3,2,1,0:T(8,128)(2,1)}, u32[]{:S(2)}, u32[]{:S(2)}) collective-permute-start(bf16[1,2,2,4,5,24,384]{6,5,4,3,2,1,0:T(8,128)(2,1)S(1)} %maximum_bitcast_fusion), channel_id=1, source_target_pairs={{0,1},{1,0},{2,3},{3,2},{4,5},{5,4},{6,7},{7,6},{8,9},{9,8},{10,11... | collective-permute-start | bytes 4423688 | tf_op jit(solution)/shard_map/ppermute | solution.py:28
  97.4 218.2 %collective-permute-start.24 = (bf16[1,2,2,4,5,24,384]{6,5,4,3,2,1,0:T(8,128)(2,1)}, bf16[1,2,2,4,5,24,384]{6,5,4,3,2,1,0:T(8,128)(2,1)}, u32[]{:S(2)}, u32[]{:S(2)}) collective-permute-start(bf16[1,2,2,4,5,24,384]{6,5,4,3,2,1,0:T(8,128)(2,1)} %maximum_bitcast_fusion.1), channel_id=1, source_target_pairs={{0,1},{1,0},{2,3},{3,2},{4,5},{5,4},{6,7},{7,6},{8,9},{9,8},{10,11... | collective-permute-start | bytes 4423688 | tf_op jit(solution)/shard_map/ppermute | solution.py:28
  498.4 152.6 %collective-permute-start.40 = (bf16[1,2,2,4,5,24,384]{6,5,4,3,2,1,0:T(8,128)(2,1)}, bf16[1,2,2,4,5,24,384]{6,5,4,3,2,1,0:T(8,128)(2,1)}, u32[]{:S(2)}, u32[]{:S(2)}) collective-permute-start(bf16[1,2,2,4,5,24,384]{6,5,4,3,2,1,0:T(8,128)(2,1)} %bitcast.154), channel_id=1, source_target_pairs={{0,1},{1,0},{2,3},{3,2},{4,5},{5,4},{6,7},{7,6},{8,9},{9,8},{10,11... | collective-permute-start | bytes 4423688 | tf_op jit(solution)/shard_map/ppermute | solution.py:28
  498.8 155.8 %collective-permute-start.45 = (bf16[1,2,2,4,5,24,384]{6,5,4,3,2,1,0:T(8,128)(2,1)}, bf16[1,2,2,4,5,24,384]{6,5,4,3,2,1,0:T(8,128)(2,1)}, u32[]{:S(2)}, u32[]{:S(2)}) collective-permute-start(bf16[1,2,2,4,5,24,384]{6,5,4,3,2,1,0:T(8,128)(2,1)} %bitcast.166), channel_id=1, source_target_pairs={{0,1},{1,0},{2,3},{3,2},{4,5},{5,4},{6,7},{7,6},{8,9},{9,8},{10,11... | collective-permute-start | bytes 4423688 | tf_op jit(solution)/shard_map/ppermute | solution.py:28
  562.9 71.3 %collective-permute-start.30 = (bf16[1,2,2,4,3,24,384]{6,5,4,3,2,1,0:T(8,128)(2,1)}, bf16[1,2,2,4,3,24,384]{6,5,4,3,2,1,0:T(8,128)(2,1)}, u32[]{:S(2)}, u32[]{:S(2)}) collective-permute-start(bf16[1,2,2,4,3,24,384]{6,5,4,3,2,1,0:T(8,128)(2,1)} %bitcast.122), channel_id=1, source_target_pairs={{0,1},{1,0},{2,3},{3,2},{4,5},{5,4},{6,7},{7,6},{8,9},{9,8},{10,11... | collective-permute-start | bytes 2654216 | tf_op jit(solution)/shard_map/ppermute | solution.py:28
  633.7 28.4 %collective-permute-start.25 = (bf16[4,2,128,768]{3,2,1,0:T(8,128)(2,1)S(1)}, bf16[4,2,128,768]{3,2,1,0:T(8,128)(2,1)S(1)}, u32[]{:S(2)}, u32[]{:S(2)}) collective-permute-start(bf16[4,2,128,768]{3,2,1,0:T(8,128)(2,1)S(1)} %bitcast.621), channel_id=1, source_target_pairs={{0,1},{1,0},{2,3},{3,2},{4,5},{5,4},{6,7},{7,6},{8,9},{9,8},{10,11... | collective-permute-start | bytes 4718600 | tf_op jit(solution)/shard_map/ppermute | solution.py:28
  653.8 59.7 %collective-permute-start.41 = (bf16[1,2,4,5,24,384]{5,4,3,2,1,0:T(8,128)(2,1)}, bf16[1,2,4,5,24,384]{5,4,3,2,1,0:T(8,128)(2,1)S(1)}, u32[]{:S(2)}, u32[]{:S(2)}) collective-permute-start(bf16[1,2,4,5,24,384]{5,4,3,2,1,0:T(8,128)(2,1)} %slice_bitcast_fusion.2), channel_id=1, source_target_pairs={{0,16},{16,0},{1,17},{17,1},{2,18},{18,2},{3,19},{19,3},{4,20},{20... | collective-permute-start | bytes 2211848 | tf_op jit(solution)/shard_map/ppermute | solution.py:28
  657.4 57.2 %collective-permute-start.46 = (bf16[1,2,4,5,24,384]{5,4,3,2,1,0:T(8,128)(2,1)}, bf16[1,2,4,5,24,384]{5,4,3,2,1,0:T(8,128)(2,1)}, u32[]{:S(2)}, u32[]{:S(2)}) collective-permute-start(bf16[1,2,4,5,24,384]{5,4,3,2,1,0:T(8,128)(2,1)} %slice_bitcast_fusion), channel_id=1, source_target_pairs={{0,2},{2,0},{1,3},{3,1},{4,6},{6,4},{5,7},{7,5},{8,10},{10,8},{9,1... | collective-permute-start | bytes 2211848 | tf_op jit(solution)/shard_map/ppermute | solution.py:28
  663.6 33.3 %collective-permute-start.26 = (bf16[2,128,768]{2,1,0:T(8,128)(2,1)}, bf16[2,128,768]{2,1,0:T(8,128)(2,1)S(1)}, u32[]{:S(2)}, u32[]{:S(2)}) collective-permute-start(bf16[2,128,768]{2,1,0:T(8,128)(2,1)} %get-tuple-element.96), channel_id=1, source_target_pairs={{0,4},{4,0},{8,12},{12,8},{1,5},{5,1},{9,13},{13,9},{2,6},{6,2},{1... | collective-permute-start | bytes 1179656 | tf_op jit(solution)/shard_map/ppermute | solution.py:28
  668.9 28.0 %collective-permute-start.28 = (bf16[2,128,768]{2,1,0:T(8,128)(2,1)}, bf16[2,128,768]{2,1,0:T(8,128)(2,1)}, u32[]{:S(2)}, u32[]{:S(2)}) collective-permute-start(bf16[2,128,768]{2,1,0:T(8,128)(2,1)} %get-tuple-element.97), channel_id=1, source_target_pairs={{0,12},{4,8},{8,4},{12,0},{1,13},{5,9},{9,5},{13,1},{2,14},{6,10},... | collective-permute-start | bytes 1179656 | tf_op jit(solution)/shard_map/ppermute | solution.py:28
  687.5 22.4 %collective-permute-start.27 = (bf16[2,128,768]{2,1,0:T(8,128)(2,1)}, bf16[2,128,768]{2,1,0:T(8,128)(2,1)}, u32[]{:S(2)}, u32[]{:S(2)}) collective-permute-start(bf16[2,128,768]{2,1,0:T(8,128)(2,1)} %get-tuple-element.98), channel_id=1, source_target_pairs={{0,8},{4,12},{8,0},{12,4},{1,9},{5,13},{9,1},{13,5},{2,10},{6,14},... | collective-permute-start | bytes 1179656 | tf_op jit(solution)/shard_map/ppermute | solution.py:28
  713.8 16.2 %collective-permute-start.42 = (bf16[1,4,5,24,384]{4,3,2,1,0:T(8,128)(2,1)S(1)}, bf16[1,4,5,24,384]{4,3,2,1,0:T(8,128)(2,1)S(1)}, u32[]{:S(2)}, u32[]{:S(2)}) collective-permute-start(bf16[1,4,5,24,384]{4,3,2,1,0:T(8,128)(2,1)S(1)} %slice_bitcast_fusion.14), channel_id=1, source_target_pairs={{0,2},{2,0},{1,3},{3,1},{4,6},{6,4},{5,7},{7,5},{8,10},{10,8},{9,1... | collective-permute-start | bytes 1105928 | tf_op jit(solution)/shard_map/ppermute | solution.py:28
  716.1 14.2 %collective-permute-start.47 = (bf16[1,4,5,24,384]{4,3,2,1,0:T(8,128)(2,1)S(1)}, bf16[1,4,5,24,384]{4,3,2,1,0:T(8,128)(2,1)S(1)}, u32[]{:S(2)}, u32[]{:S(2)}) collective-permute-start(bf16[1,4,5,24,384]{4,3,2,1,0:T(8,128)(2,1)S(1)} %slice_bitcast_fusion.12), channel_id=1, source_target_pairs={{0,16},{16,0},{1,17},{17,1},{2,18},{18,2},{3,19},{19,3},{4,20},{20... | collective-permute-start | bytes 1105928 | tf_op jit(solution)/shard_map/ppermute | solution.py:28
  730.1 15.3 %collective-permute-start.43 = (bf16[2,5,24,384]{3,2,1,0:T(8,128)(2,1)S(1)}, bf16[2,5,24,384]{3,2,1,0:T(8,128)(2,1)S(1)}, u32[]{:S(2)}, u32[]{:S(2)}) collective-permute-start(bf16[2,5,24,384]{3,2,1,0:T(8,128)(2,1)S(1)} %slice_bitcast_fusion.24), channel_id=1, source_target_pairs={{0,8},{4,12},{8,0},{12,4},{1,9},{5,13},{9,1},{13,5},{2,10},{6,14},... | collective-permute-start | bytes 552968 | tf_op jit(solution)/shard_map/ppermute | solution.py:28
  730.4 17.1 %collective-permute-start.48 = (bf16[2,5,24,384]{3,2,1,0:T(8,128)(2,1)S(1)}, bf16[2,5,24,384]{3,2,1,0:T(8,128)(2,1)S(1)}, u32[]{:S(2)}, u32[]{:S(2)}) collective-permute-start(bf16[2,5,24,384]{3,2,1,0:T(8,128)(2,1)S(1)} %slice_bitcast_fusion.22), channel_id=1, source_target_pairs={{0,8},{4,12},{8,0},{12,4},{1,9},{5,13},{9,1},{13,5},{2,10},{6,14},... | collective-permute-start | bytes 552968 | tf_op jit(solution)/shard_map/ppermute | solution.py:28
  (143 other events, 1353.9 us)
